TPU v7x, 32 devices: a whole 2x2x4 slice. The times are simulated.
32 devices in a mesh: member: 4 (over z), lat: 4 (over y, core), lon: 2 (over x).
Axes of the slice: x: 2, y: 2, z: 4, core: 2. Of those that a mesh axis runs over, the one named last changes fastest.
Arguments:
- fields: float32 [8, 32, 160, 1024], P('member', None, 'lat', 'lon'), may hold values from -6 to 6
- spectra: float32 [9, 513], replicated, may hold values from 0.3 to 1.5
- band_weights: float32 [9, 160, 5], P(None, 'lat'), may hold values from -2.5 to 2.5
- band_start: int32 [160], P('lat'), may hold values from 0 to 155, as said below
- depth_weights: float32 [32, 9], replicated, may hold values from -2 to 2
- mix_weights: float32 [32, 32], replicated, may hold values from -1 to 1
- target: float32 [32, 160, 1024], P('member', 'lat', 'lon'), may hold values from -6 to 6
Outputs:
- crps: float32 [32, 160, 1024], P('member', 'lat', 'lon')
Inputs may be any that keep to these rules, and one draw needn't show every extreme that they name: For each output row o, band_start[o] lies between o - 5 and o + 5 - 5 + 1; both ends of that offset range occur.
All inputs are finite; a program needn't handle non-finite values.
Results may differ from a plain program's by a relative error of at most 0.0001.
Values sent between devices are 32-bit elements; how exact they have to be, the bound alone decides.
A program may use at most 128 MiB of HBM per device.

v0:
```python
import math

import jax
import jax.numpy as jnp
from jax import lax
from jax.sharding import PartitionSpec as P

REACH = 5


def with_halo(value, sides, width):
    for axis, dim in sides:
        size, length = (lax.axis_size(axis), value.shape[dim])
        up = [(i, (i + 1) % size) for i in range(size - 1)]
        down = [(j, i) for i, j in up]
        last = lax.slice_in_dim(value, length - width, length, axis=dim)
        first = lax.slice_in_dim(value, 0, width, axis=dim)
        before = lax.ppermute(last, axis, up)
        after = lax.ppermute(first, axis, down)
        value = jnp.concatenate([before, value, after], axis=dim)
    return value


def forward_table(length, start_col, num_cols):
    half_len = length // 2
    column = start_col + jnp.arange(num_cols, dtype=jnp.int32)
    is_cosine = column <= half_len
    frequency = jnp.where(is_cosine, column, column - half_len)
    cell_idx = jnp.arange(length, dtype=jnp.int32)
    phase_int = cell_idx[:, None] * frequency[None, :] % length
    angle_rad = phase_int.astype(jnp.float32) * (2.0 * math.pi / length)
    return jnp.where(is_cosine[None, :], jnp.cos(angle_rad), jnp.sin(angle_rad))


def inverse_table(length, start_col, num_cols):
    half_len = length // 2
    column = jnp.arange(length, dtype=jnp.int32)
    is_cosine = column <= half_len
    frequency = jnp.where(is_cosine, column, column - half_len)
    cell_idx = start_col + jnp.arange(num_cols, dtype=jnp.int32)
    phase_int = frequency[:, None] * cell_idx[None, :] % length
    angle_rad = phase_int.astype(jnp.float32) * (2.0 * math.pi / length)
    edge_freq = jnp.logical_and(is_cosine, jnp.logical_or(frequency == 0, frequency == half_len))
    synth_scale = jnp.where(edge_freq, 1.0, 2.0) / length
    return (
        jnp.where(is_cosine[:, None], jnp.cos(angle_rad), jnp.sin(angle_rad)) * synth_scale[:, None]
    )


def apply_blocks(values, table_maker):
    dims_in = values.shape
    length = dims_in[-1]
    flat_rows = values.reshape(-1, length)
    piece_width = length // 8
    pieces = []
    for segment in range(8):
        basis_table = table_maker(length, segment * piece_width, piece_width)
        pieces.append(
            jnp.dot(
                flat_rows,
                basis_table,
                precision=lax.Precision.HIGHEST,
                preferred_element_type=jnp.float32,
            )
        )
    return jnp.concatenate(pieces, axis=1).reshape(dims_in)


def analyse(values):
    return apply_blocks(values, forward_table)


def synthesise(values):
    return apply_blocks(values, inverse_table)


def pair_total(ensemble):

    def step(member_idx, acc_sum):
        picked = lax.dynamic_index_in_dim(ensemble, member_idx, 0, keepdims=True)
        return acc_sum + jnp.sum(jnp.abs(picked - ensemble), axis=0)

    start_sum = jnp.zeros(ensemble.shape[1:], jnp.float32)
    return lax.fori_loop(0, ensemble.shape[0], step, start_sum)


def score_cells(ensemble, analysis):
    total_members = ensemble.shape[0]
    skill_term = jnp.mean(jnp.abs(ensemble - analysis[None]), axis=0)
    spread = pair_total(ensemble)
    return skill_term - spread / (2.0 * total_members * total_members)


def mix_tiles(in_tiles, mix_weights, n_member, n_lon, own_vars):
    variables = mix_weights.shape[0]
    reordered = (
        mix_weights.reshape(variables, n_member, n_lon, own_vars)
        .transpose(0, 2, 1, 3)
        .reshape(variables, variables)
    )
    mixed_out = jnp.einsum("dc,mcal->mdal", reordered, in_tiles, precision=lax.Precision.HIGHEST)
    return jax.nn.gelu(mixed_out, approximate=False)


def local(fields, spectra, band_weights, band_start, depth_weights, mix_weights, target):
    lat_rows = fields.shape[2]
    n_basis = spectra.shape[0]
    band_len = band_weights.shape[2]
    n_member = lax.axis_size("member")
    n_lon = lax.axis_size("lon")
    circles = lax.all_to_all(
        lax.all_to_all(fields, "member", split_axis=1, concat_axis=0, tiled=True),
        "lon",
        split_axis=1,
        concat_axis=3,
        tiled=True,
    )
    members = circles.shape[0]
    own_vars = circles.shape[1]
    length = circles.shape[3]
    extended = with_halo(analyse(circles), (("lat", 2),), REACH)
    ext_rows = lat_rows + 2 * REACH
    first_row = lax.axis_index("lat") * lat_rows
    local_start = band_start - first_row + REACH
    read_rows = local_start[:, None] + jnp.arange(band_len, dtype=jnp.int32)[None, :]
    matches = (
        read_rows[:, :, None] == jnp.arange(ext_rows, dtype=jnp.int32)[None, None, :]
    ).astype(jnp.float32)
    selector = jnp.einsum("koj,oji->koi", band_weights, matches, precision=lax.Precision.HIGHEST)
    half_spec = jnp.concatenate([spectra, spectra[:, 1:-1]], axis=1)
    var_start = lax.axis_index("member") * (own_vars * n_lon) + lax.axis_index("lon") * own_vars
    depth_slice = lax.dynamic_slice_in_dim(depth_weights, var_start, own_vars, 0)
    summed = jnp.zeros((members, own_vars, lat_rows, length), jnp.float32)
    for basis_idx in range(n_basis):
        banded = jnp.einsum(
            "oi,mcif->mcof", selector[basis_idx], extended, precision=lax.Precision.HIGHEST
        )
        factor = (
            depth_slice[:, basis_idx][None, :, None, None]
            * half_spec[basis_idx][None, None, None, :]
        )
        summed = summed + factor * banded
    smooth = synthesise(summed)
    in_tiles = lax.all_to_all(
        lax.all_to_all(smooth, "member", split_axis=0, concat_axis=1, tiled=True),
        "lon",
        split_axis=3,
        concat_axis=1,
        tiled=True,
    )
    hidden = mix_tiles(in_tiles, mix_weights, n_member, n_lon, own_vars)
    ensemble = lax.all_to_all(hidden, "member", split_axis=1, concat_axis=0, tiled=True)
    return score_cells(ensemble, target)


def solution(mesh):
    in_specs = (
        P("member", None, "lat", "lon"),
        P(),
        P(None, "lat", None),
        P("lat"),
        P(),
        P(),
        P("member", "lat", "lon"),
    )
    out_specs = P("member", "lat", "lon")
    return jax.shard_map(local, mesh=mesh, in_specs=in_specs, out_specs=out_specs, check_vma=False)
```

profile of v0, /device:TPU:1, one launch (start us, length us, event | category | flops | bytes accessed | tf_op | source)
XLA Modules:
  0.0 948.3 jit_solution(414945144375338798)
XLA Ops:
  11.3 115.5 %all-to-all-done = f32[2,32,40,512]{3,2,0,1:T(8,128)} async-done(((f32[2,32,40,512]{3,2,0,1:T(8,128)}), f32[2,32,40,512]{3,2,0,1:T(8,128)}, u32[]{:S(2)}, u32[]{:S(2)}) %all-to-all-start) | async-done | bytes 5242912 | tf_op jit(solution)/shard_map/all_to_all | solution.py:112
  140.2 56.3 %all-to-all-done.1 = f32[8,8,40,512]{3,2,0,1:T(8,128)} async-done(((f32[8,8,40,512]{3,2,0,1:T(8,128)}), f32[8,8,40,512]{3,2,0,1:T(8,128)}, u32[]{:S(2)}, u32[]{:S(2)}) %all-to-all-start.1) | async-done | bytes 5242912 | tf_op jit(solution)/shard_map/all_to_all | solution.py:111
  291.8 10.1 %fusion.400 = f32[8,4,1024,40]{2,3,1,0:T(8,128)} fusion(f32[40,50,1,1]{1,0,3,2:T(8,128)S(1)} %bitcast.284, f32[8,4,5,1024]{3,2,1,0:T(8,128)S(1)} %copy.47, f32[8,4,40,1024]{3,2,1,0:T(8,128)S(1)} %bitcast.250, f32[8,4,5,1024]{3,2,1,0:T(8,128)S(1)} %copy.46), kind=kOutput, calls=%fused_computation.511 | convolution fusion | flops 789708800 | bytes 11804480 | tf_op jit(solution)/shard_map/oi,mcif->mcof/dot_general | solution.py:135
  301.9 10.2 %fusion.399 = f32[8,4,1024,40]{2,3,1,0:T(8,128)} fusion(f32[40,50,1,1]{1,0,3,2:T(8,128)S(1)} %bitcast.283, f32[8,4,5,1024]{3,2,1,0:T(8,128)S(1)} %copy.47, f32[8,4,40,1024]{3,2,1,0:T(8,128)S(1)} %bitcast.251, f32[8,4,5,1024]{3,2,1,0:T(8,128)S(1)} %copy.46), kind=kOutput, calls=%fused_computation.510 | convolution fusion | flops 789708800 | bytes 11804480 | tf_op jit(solution)/shard_map/oi,mcif->mcof/dot_general | solution.py:135
  312.1 10.2 %fusion.398 = f32[8,4,1024,40]{2,3,1,0:T(8,128)} fusion(f32[40,50,1,1]{1,0,3,2:T(8,128)S(1)} %bitcast.282, f32[8,4,5,1024]{3,2,1,0:T(8,128)S(1)} %copy.47, f32[8,4,40,1024]{3,2,1,0:T(8,128)S(1)} %bitcast.252, f32[8,4,5,1024]{3,2,1,0:T(8,128)S(1)} %copy.46), kind=kOutput, calls=%fused_computation.509 | convolution fusion | flops 789708800 | bytes 11804480 | tf_op jit(solution)/shard_map/oi,mcif->mcof/dot_general | solution.py:135
  322.3 10.3 %fusion.397 = f32[8,4,1024,40]{2,3,1,0:T(8,128)} fusion(f32[40,50,1,1]{1,0,3,2:T(8,128)S(1)} %bitcast.281, f32[8,4,5,1024]{3,2,1,0:T(8,128)S(1)} %copy.47, f32[8,4,40,1024]{3,2,1,0:T(8,128)S(1)} %bitcast.253, f32[8,4,5,1024]{3,2,1,0:T(8,128)S(1)} %copy.46), kind=kOutput, calls=%fused_computation.508 | convolution fusion | flops 789708800 | bytes 11804480 | tf_op jit(solution)/shard_map/oi,mcif->mcof/dot_general | solution.py:135
  332.7 10.1 %fusion.396 = f32[8,4,1024,40]{2,3,1,0:T(8,128)} fusion(f32[40,50,1,1]{1,0,3,2:T(8,128)S(1)} %bitcast.280, f32[8,4,5,1024]{3,2,1,0:T(8,128)S(1)} %copy.47, f32[8,4,40,1024]{3,2,1,0:T(8,128)S(1)} %bitcast.254, f32[8,4,5,1024]{3,2,1,0:T(8,128)S(1)} %copy.46), kind=kOutput, calls=%fused_computation.507 | convolution fusion | flops 789708800 | bytes 11804480 | tf_op jit(solution)/shard_map/oi,mcif->mcof/dot_general | solution.py:135
  342.8 10.1 %fusion.395 = f32[8,4,1024,40]{2,3,1,0:T(8,128)} fusion(f32[40,50,1,1]{1,0,3,2:T(8,128)S(1)} %bitcast.279, f32[8,4,5,1024]{3,2,1,0:T(8,128)S(1)} %copy.47, f32[8,4,40,1024]{3,2,1,0:T(8,128)S(1)} %bitcast.255, f32[8,4,5,1024]{3,2,1,0:T(8,128)S(1)} %copy.46), kind=kOutput, calls=%fused_computation.506 | convolution fusion | flops 789708800 | bytes 11804480 | tf_op jit(solution)/shard_map/oi,mcif->mcof/dot_general | solution.py:135
  352.9 10.5 %fusion.394 = f32[8,4,1024,40]{2,3,1,0:T(8,128)} fusion(f32[40,50,1,1]{1,0,3,2:T(8,128)S(1)} %bitcast.278, f32[8,4,5,1024]{3,2,1,0:T(8,128)S(1)} %copy.47, f32[8,4,40,1024]{3,2,1,0:T(8,128)S(1)} %bitcast.256, f32[8,4,5,1024]{3,2,1,0:T(8,128)S(1)} %copy.46), kind=kOutput, calls=%fused_computation.505 | convolution fusion | flops 789708800 | bytes 11804480 | tf_op jit(solution)/shard_map/oi,mcif->mcof/dot_general | solution.py:135
  363.4 10.2 %fusion.393 = f32[8,4,1024,40]{2,3,1,0:T(8,128)} fusion(f32[40,50,1,1]{1,0,3,2:T(8,128)S(1)} %bitcast.277, f32[8,4,5,1024]{3,2,1,0:T(8,128)S(1)} %copy.47, f32[8,4,40,1024]{3,2,1,0:T(8,128)S(1)} %bitcast.257, f32[8,4,5,1024]{3,2,1,0:T(8,128)S(1)} %copy.46), kind=kOutput, calls=%fused_computation.504 | convolution fusion | flops 789708800 | bytes 11804480 | tf_op jit(solution)/shard_map/oi,mcif->mcof/dot_general | solution.py:135
  373.6 24.1 %add_add_fusion = f32[8,4,1024,40]{2,3,1,0:T(8,128)} fusion(f32[8,4,1024,40]{2,3,1,0:T(8,128)} %fusion.393, f32[8,4,1024,40]{2,3,1,0:T(8,128)} %fusion.394, f32[8,4,1024,40]{2,3,1,0:T(8,128)} %fusion.395, f32[8,4,1024,40]{2,3,1,0:T(8,128)} %fusion.396, f32[8,4,1024,40]{2,3,1,0:T(8,128)} %fusion.397, f32[8,4,1024,40]{2,3,1,0:T(8,128)} %fusion.398, ...), kind=kOutput, calls=%fused_computation.15 | convolution fusion | flops 811991040 | bytes 53894976 | tf_op jit(solution)/shard_map/oi,mcif->mcof/dot_general | solution.py:135
  397.8 11.3 %convolution_dynamic-update-slice_fusion.7 = f32[1280,1024]{0,1:T(8,128)} fusion(f32[1280,1024]{1,0:T(8,128)} %bitcast.240, f32[1024]{0:T(1024)S(1)} %select_multiply_fusion, s32[1024]{0:T(1024)S(1)} %add_select_fusion.16, pred[1024]{0:T(1024)(128)(4,1)S(1)} %iota_compare_fusion.2), kind=kOutput, calls=%fused_computation.38 | convolution fusion | flops 2015363072 | bytes 5907456 | tf_op jit(solution)/shard_map/dot_general | solution.py:59
  416.8 8.2 convolution_dynamic-update-slice_fusion.5
  448.4 8.2 convolution_dynamic-update-slice_fusion.1
  470.3 112.5 %all_to_all.87 = f32[8,4,40,1024]{3,2,1,0:T(8,128)S(1)} all-to-all(f32[8,4,40,1024]{3,2,1,0:T(8,128)} %bitcast.271), channel_id=1, replica_groups=mesh['member'=4,'lat'=4,'lon'=2] {'member'}, dimensions={0} | all-to-all | bytes 10485760 | tf_op jit(solution)/shard_map/all_to_all | solution.py:145
  585.7 14.7 %copy.51 = f32[2,16,40,1024]{2,1,0,3:T(8,128)} copy(f32[2,16,40,1024]{3,2,1,0:T(8,128)} %bitcast.273) | data formatting | bytes 10485760 | tf_op jit(solution)/shard_map/all_to_all | solution.py:145
  600.4 24.8 %reshape.487 = f32[2,1,655360]{2,1,0:T(1,128)} reshape(f32[1024,2,16,40]{3,2,1,0:T(8,128)} %bitcast.267) | data formatting | bytes 10485760
  631.4 56.8 %all-to-all-done.3 = f32[2,1,655360]{2,1,0:T(1,128)} async-done(((f32[2,1,655360]{2,1,0:T(1,128)}), f32[2,1,655360]{2,1,0:T(1,128)}, u32[]{:S(2)}, u32[]{:S(2)}) %all-to-all-start.3) | async-done | bytes 5242912 | tf_op jit(solution)/shard_map/all_to_all | solution.py:144
  688.7 19.6 %reduce.1 = f32[2,655360]{1,0:T(2,128)} reduce(f32[2,1,655360]{2,1,0:T(1,128)} %all-to-all-done.3, f32[]{:T(128)} %broadcast.758), dimensions={1}, to_apply=%all_to_all.74.reduce_sub_computation | reduce | bytes 10485764 | tf_op jit(solution)/shard_map/all_to_all | solution.py:144
  708.3 23.1 %reshape.488 = f32[1024,2,16,40]{3,2,1,0:T(8,128)} reshape(f32[2,655360]{1,0:T(2,128)} %reduce.1) | data formatting | bytes 10485760
  731.4 15.5 %copy.74 = f32[2,16,40,2,512]{4,3,2,1,0:T(2,128)} copy(f32[2,16,40,2,512]{2,1,0,4,3:T(8,128)} %bitcast.268) | data formatting | bytes 10485760 | tf_op jit(solution)/shard_map/all_to_all | solution.py:144
  752.5 18.8 %fusion.1 = f32[2,32,40,512]{3,1,2,0:T(8,128)S(1)} fusion(f32[2,32,40,512]{3,1,2,0:T(8,128)S(1)} %bitcast.275, f32[32,32,1,1]{0,1,3,2:T(8,128)S(1)} %bitcast.295), kind=kOutput, calls=%fused_computation.6 | convolution fusion | flops 587202560 | bytes 10489856 | tf_op jit(solution)/shard_map/dc,mcal->mdal/dot_general | solution.py:101
  782.4 114.6 %all-to-all-done.4 = f32[2,32,40,512]{3,2,0,1:T(8,128)} async-done(((f32[2,32,40,512]{3,2,0,1:T(8,128)}), f32[2,32,40,512]{3,2,0,1:T(8,128)}, u32[]{:S(2)}, u32[]{:S(2)}) %all-to-all-start.4) | async-done | bytes 5242912 | tf_op jit(solution)/shard_map/all_to_all | solution.py:152
  902.7 37.6 %while.14 = (s32[]{:T(128)}, f32[8,40,512]{2,1,0:T(8,128)S(1)}, f32[8,8,40,512]{3,2,1,0:T(8,128)}, s32[]{:T(128)}, s32[]{:T(128)}) while((s32[]{:T(128)}, f32[8,40,512]{2,1,0:T(8,128)S(1)}, f32[8,8,40,512]{3,2,1,0:T(8,128)}, s32[]{:T(128)}, s32[]{:T(128)}) %tuple.64), condition=%wide.region_3.4_spmd.clone, body=%wide.region_1.3_spmd.clone.sunk | while | flops 4096003 | bytes 9830475 | solution.py:84
  (124 shorter events, 241.8 us)
Async XLA Ops:
  5.7 121.1 %all-to-all-start = ((f32[2,32,40,512]{3,2,0,1:T(8,128)}), f32[2,32,40,512]{3,2,0,1:T(8,128)}, u32[]{:S(2)}, u32[]{:S(2)}) async-start(f32[2,32,40,512]{3,2,0,1:T(8,128)} %copy.38), calls=%async_computation | async-start | bytes 10485760 | tf_op jit(solution)/shard_map/all_to_all | solution.py:112
  132.8 6.4 copy-start.4
  132.8 6.6 copy-start.3
  132.8 6.8 copy-start.6
  132.8 7.0 copy-start.7
  132.8 63.6 %all-to-all-start.1 = ((f32[8,8,40,512]{3,2,0,1:T(8,128)}), f32[8,8,40,512]{3,2,0,1:T(8,128)}, u32[]{:S(2)}, u32[]{:S(2)}) async-start(f32[8,8,40,512]{3,2,0,1:T(8,128)} %copy.41), calls=%async_computation.1 | async-start | bytes 10485760 | tf_op jit(solution)/shard_map/all_to_all | solution.py:111
  271.4 20.4 %copy-start.1 = (f32[1280,1024]{1,0:T(8,128)S(1)}, f32[1280,1024]{1,0:T(8,128)}, u32[]{:S(2)}) copy-start(f32[1280,1024]{1,0:T(8,128)} %copy.43) | copy-start | bytes 15728644
  273.7 12.9 %collective-permute-start = (f32[8,4,5,1024]{3,0,2,1:T(8,128)S(1)}, f32[8,4,5,1024]{3,0,2,1:T(8,128)S(1)}, u32[]{:S(2)}, u32[]{:S(2)}) collective-permute-start(f32[8,4,5,1024]{3,0,2,1:T(8,128)S(1)} %copy.44), channel_id=1, source_target_pairs={{0,2},{2,4},{4,6},{1,3},{3,5},{5,7},{8,10},{10,12},{12,14},{9,11},... | collective-permute-start | bytes 1966088 | tf_op jit(solution)/shard_map/ppermute | solution.py:18
  279.5 11.9 %collective-permute-start.1 = (f32[8,4,5,1024]{3,0,2,1:T(8,128)S(1)}, f32[8,4,5,1024]{3,0,2,1:T(8,128)S(1)}, u32[]{:S(2)}, u32[]{:S(2)}) collective-permute-start(f32[8,4,5,1024]{3,0,2,1:T(8,128)S(1)} %copy.45), channel_id=1, source_target_pairs={{2,0},{4,2},{6,4},{3,1},{5,3},{7,5},{10,8},{12,10},{14,12},{11,9},... | collective-permute-start | bytes 1966088 | tf_op jit(solution)/shard_map/ppermute | solution.py:19
  397.8 11.3 %copy-start = (f32[8,4,1024,40]{2,3,1,0:T(8,128)S(1)}, f32[8,4,1024,40]{2,3,1,0:T(8,128)}, u32[]{:S(2)}) copy-start(f32[8,4,1024,40]{2,3,1,0:T(8,128)} %add_add_fusion) | copy-start | bytes 15728644
  625.2 6.1 copy-start.5
  625.2 63.0 %all-to-all-start.3 = ((f32[2,1,655360]{2,1,0:T(1,128)}), f32[2,1,655360]{2,1,0:T(1,128)}, u32[]{:S(2)}, u32[]{:S(2)}) async-start(f32[2,1,655360]{2,1,0:T(1,128)} %reshape.487), calls=%async_computation.3 | async-start | bytes 10485760 | tf_op jit(solution)/shard_map/all_to_all | solution.py:144
  776.6 5.4 copy-start.2
  776.6 120.4 %all-to-all-start.4 = ((f32[2,32,40,512]{3,2,0,1:T(8,128)}), f32[2,32,40,512]{3,2,0,1:T(8,128)}, u32[]{:S(2)}, u32[]{:S(2)}) async-start(f32[2,32,40,512]{3,2,0,1:T(8,128)} %copy.57), calls=%async_computation.4 | async-start | bytes 10485760 | tf_op jit(solution)/shard_map/all_to_all | solution.py:152
where the time goes:
time: 953 us; the launch traced here: 948 us
  waiting for transfers between devices  352 us (37%)
  matrix products  253 us (27%)
  local copies, waits for them, and re-layouts  144 us (15%)
  blocking collectives  112 us (12%)
  other arithmetic  55.1 us (6%)
  starting transfers between devices  30.6 us (3%)
    dot_general x16, matrix products, apply_blocks(): jnp.dot(flat_rows, basis_table, precision=lax.Precision.HIGHEST, preferre...  128 us
    all_to_all x1, waiting for transfers between devices, local(): lax.all_to_all(fields, 'member', split_axis=1, concat_axis=0, tiled=True)  115 us
    all_to_all x1, waiting for transfers between devices, local(): lax.all_to_all(hidden, 'member', split_axis=1, concat_axis=0, tiled=True)  115 us
    all_to_all x1, blocking collectives, local(): lax.all_to_all(smooth, 'member', split_axis=0, concat_axis=1, tiled=True)  112 us
    dot_general x9, matrix products, local(): jnp.einsum('oi,mcif->mcof', selector[basis_idx], extended, precision=lax....  106 us
    all_to_all x1, waiting for transfers between devices, local(): lax.all_to_all(lax.all_to_all(smooth, 'member', split_axis=0, concat_axis...  56.8 us
    all_to_all x1, waiting for transfers between devices, local(): lax.all_to_all(lax.all_to_all(fields, 'member', split_axis=1, concat_axis...  56.3 us
    unnamed x23, local copies, waits for them, and re-layouts  55.5 us
  transfers between devices with their start and end apart: 6, of which 6 were waited for; matrix products, arithmetic and copies ran while one was open for 0% of the time, Pallas kernels for 0%

commit v1 on v0

v1 whole, which is shorter than its diff:
```python
import functools
import math

import jax
import jax.numpy as jnp
import numpy as np
from jax import lax
from jax.experimental import pallas as pl
from jax.experimental.pallas import tpu as pltpu
from jax.sharding import PartitionSpec as P

REACH = 5
CHUNK = 8
HIGH = lax.Precision.HIGH


def tables(length):
    half = length // 2
    column = np.arange(length)
    is_cosine = column <= half
    frequency = np.where(is_cosine, column, column - half)
    angle = (np.arange(length)[:, None] * frequency[None, :] % length) * (2.0 * math.pi / length)
    forward = np.where(is_cosine[None, :], np.cos(angle), np.sin(angle))
    edge = is_cosine & ((frequency == 0) | (frequency == half))
    inverse = (forward * np.where(edge, 1.0, 2.0)[None, :] / length).T
    return forward.astype(np.float32), inverse.astype(np.float32)


def shifted(value, axis, shift):
    size = lax.axis_size(axis)
    return lax.ppermute(value, axis, [(i, (i + shift) % size) for i in range(size)])


def band_kernel(n_basis, band_len, starts_ref, weights_ref, factor_ref, *refs):
    rows, out_ref = refs[:band_len], refs[band_len]
    row = pl.program_id(0)
    members, length = out_ref.shape[1], out_ref.shape[3]
    scalars = [
        [weights_ref[(row * n_basis + k) * band_len + j] for j in range(band_len)]
        for k in range(n_basis)
    ]
    width = 128
    for tile in range(length // width):
        lanes = pl.ds(tile * width, width)
        gains = [None] * band_len
        for k in range(n_basis):
            factor = factor_ref[k, :, lanes]
            for j in range(band_len):
                term = scalars[k][j] * factor
                gains[j] = term if k == 0 else gains[j] + term
        for m in range(members):
            total = gains[0] * rows[0][0, m, :, lanes]
            for j in range(1, band_len):
                total = total + gains[j] * rows[j][0, m, :, lanes]
            out_ref[0, m, :, lanes] = total


def band_rows(source, starts, weights, factor):
    n_basis, n_rows, band_len = weights.shape
    _, members, own, length = source.shape
    flat = weights.transpose(1, 0, 2).reshape(-1)

    def pick(j):
        return pl.BlockSpec((1, members, own, length), lambda o, s: (s[o] + j, 0, 0, 0))

    return pl.pallas_call(
        functools.partial(band_kernel, n_basis, band_len),
        grid_spec=pltpu.PrefetchScalarGridSpec(
            num_scalar_prefetch=1,
            grid=(n_rows,),
            in_specs=[
                pl.BlockSpec(memory_space=pltpu.SMEM),
                pl.BlockSpec(factor.shape, lambda o, s: (0, 0, 0)),
            ]
            + [pick(j) for j in range(band_len)],
            out_specs=pl.BlockSpec((1, members, own, length), lambda o, s: (o, 0, 0, 0)),
        ),
        out_shape=jax.ShapeDtypeStruct((n_rows, members, own, length), jnp.float32),
        compiler_params=pltpu.CompilerParams(vmem_limit_bytes=16 * 1024 * 1024),
        cost_estimate=pl.CostEstimate(
            flops=2 * n_rows * own * length * band_len * (n_basis + members) * 16,
            bytes_accessed=4 * n_rows * (band_len + 1) * members * own * length,
            transcendentals=0,
        ),
    )(starts, flat, factor, *([source] * band_len))


def score(pieces, analysis):
    ensemble = [p[:, m] for p in pieces for m in range(p.shape[1])]
    count = len(ensemble)
    skill = sum(jnp.abs(h - analysis) for h in ensemble) / count
    spread = sum(
        jnp.abs(ensemble[i] - ensemble[j]) for i in range(count) for j in range(i + 1, count)
    )
    return skill - spread / (count * count)


def local(fields, spectra, band_weights, band_start, depth_weights, mix_weights, target):
    members, variables, n_rows, seg = fields.shape
    n_lon, n_member = lax.axis_size("lon"), lax.axis_size("member")
    lon, me = lax.axis_index("lon"), lax.axis_index("member")
    own, group = variables // n_lon, variables // n_member
    length = seg * n_lon
    forward, inverse = tables(length)
    forward = jnp.asarray(forward.reshape(n_lon, seg, length))
    inverse = jnp.asarray(np.ascontiguousarray(inverse.reshape(length, n_lon, seg).transpose(1, 0, 2)))

    def at(value, index, axis=0):
        return lax.dynamic_index_in_dim(value, index, axis, keepdims=False)

    by_owner = fields.reshape(members, n_lon, own, n_rows, seg)
    spectrum = None
    for s in range(n_lon):
        piece = at(by_owner, (lon + s) % n_lon, 1).transpose(2, 0, 1, 3)
        if s > 0:
            piece = shifted(piece, "lon", s)
        part = jnp.dot(
            piece.reshape(-1, seg),
            at(forward, (lon + n_lon - s) % n_lon),
            precision=HIGH,
            preferred_element_type=jnp.float32,
        )
        spectrum = part if spectrum is None else spectrum + part
    spectrum = spectrum.reshape(n_rows, members, own, length)

    size = lax.axis_size("lat")
    up = [(i, i + 1) for i in range(size - 1)]
    before = lax.ppermute(spectrum[n_rows - REACH :], "lat", up)
    after = lax.ppermute(spectrum[:REACH], "lat", [(j, i) for i, j in up])

    half_spec = jnp.concatenate([spectra, spectra[:, 1:-1]], axis=1)
    depth_own = lax.dynamic_slice_in_dim(depth_weights, lon * own, own, 0)
    factor = depth_own.T[:, :, None] * half_spec[:, None, :]
    starts = band_start - lax.axis_index("lat") * n_rows

    chunk = CHUNK if n_rows % CHUNK == 0 else n_rows
    rm = chunk * members
    mix_rolled = jnp.stack(
        [at(mix_weights.reshape(n_member, group, variables), (me + s) % n_member) for s in range(n_member)]
    ).reshape(n_member, group, n_lon, own)
    eye = jnp.eye(rm, dtype=jnp.float32)
    mixers = []
    for s in range(n_lon):
        block = at(mix_rolled, (lon + n_lon - s) % n_lon, 2)
        wide = block[:, None, :, None, :] * eye[None, :, None, :, None]
        mixers.append(wide.reshape(n_member * rm * group, rm * own))
    inverse_seg = [at(inverse, (lon + s) % n_lon) for s in range(n_lon)]

    chunks = n_rows // chunk
    inner = [q for q in range(chunks) if q * chunk >= REACH and (q + 1) * chunk + REACH <= n_rows]
    order = inner + [q for q in range(chunks) if q not in inner]
    results = [None] * chunks
    for q in order:
        low, high = q * chunk, (q + 1) * chunk
        first = 0
        source = spectrum
        if q not in inner:
            first, last = max(low - REACH, 0), min(high + REACH, n_rows)
            parts = [spectrum[first:last]]
            if low < REACH:
                parts, first = [before] + parts, -REACH
            if high + REACH > n_rows:
                parts = parts + [after]
            source = jnp.concatenate(parts, axis=0)
        filtered = band_rows(source, starts[low:high] - first, band_weights[:, low:high], factor)
        filtered = filtered.reshape(rm * own, length)
        mixed = None
        for s in range(n_lon):
            smooth = jnp.dot(
                filtered, inverse_seg[s], precision=HIGH, preferred_element_type=jnp.float32
            )
            if s > 0:
                smooth = shifted(smooth, "lon", s)
            part = jnp.dot(mixers[s], smooth, precision=HIGH, preferred_element_type=jnp.float32)
            mixed = part if mixed is None else mixed + part
        hidden = jax.nn.gelu(mixed, approximate=False)
        hidden = hidden.reshape(n_member, chunk, members, group, seg)
        pieces = [hidden[0]] + [shifted(hidden[s], "member", s) for s in range(1, n_member)]
        analysis = target[:, low:high].transpose(1, 0, 2)
        results[q] = score(pieces, analysis).transpose(1, 0, 2)
    return jnp.concatenate(results, axis=1)


def solution(mesh):
    in_specs = (
        P("member", None, "lat", "lon"),
        P(),
        P(None, "lat", None),
        P("lat"),
        P(),
        P(),
        P("member", "lat", "lon"),
    )
    out_specs = P("member", "lat", "lon")
    return jax.shard_map(local, mesh=mesh, in_specs=in_specs, out_specs=out_specs, check_vma=False)
```

time: 953 us -> 290 us (0.30)
  the two profiles are of different devices: /device:TPU:1 before, /device:TPU:13 now
where the time goes in v1:
time: 290 us; the launch traced here: 285 us
  waiting for transfers between devices  139 us (48%)
  matrix products  60.3 us (21%)
  starting transfers between devices  35.8 us (12%)
  local copies, waits for them, and re-layouts  24.2 us (8%)
  Pallas kernels  16.8 us (6%)
  other arithmetic  8.57 us (3%)
    ppermute x21, waiting for transfers between devices, shifted(): lax.ppermute(value, axis, [(i, (i + shift) % size) for i in range(size)])  139 us
    dot_general x10, matrix products, local(): jnp.dot(mixers[s], smooth, precision=HIGH, preferred_element_type=jnp.flo...  35.5 us
    ppermute x21, starting transfers between devices, shifted(): lax.ppermute(value, axis, [(i, (i + shift) % size) for i in range(size)])  29.6 us
    pallas_call x5, Pallas kernels, band_rows(): pl.pallas_call(functools.partial(band_kernel, n_basis, band_len), grid_sp...  16.8 us
    dot_general x2, matrix products, local(): jnp.dot(piece.reshape(-1, seg), at(forward, (lon + n_lon - s) % n_lon), p...  12.6 us
    dot_general x10, matrix products, local(): jnp.dot(filtered, inverse_seg[s], precision=HIGH, preferred_element_type=...  12.2 us
    mul x2, local copies, waits for them, and re-layouts, local(): wide = block[:, None, :, None, :] * eye[None, :, None, :, None]  8.21 us
    unnamed x24, local copies, waits for them, and re-layouts  6.31 us
  transfers between devices with their start and end apart: 23, of which 15 were waited for; matrix products, arithmetic and copies ran while one was open for 25% of the time, Pallas kernels for 2%

profile of v1, /device:TPU:13, one launch (start us, length us, event | category | flops | bytes accessed | tf_op | source)
XLA Modules:
  0.0 285.5 jit_solution(1314561590942648486)
XLA Ops:
  0.0 4.6 %constant_dynamic-slice_fusion.1 = (f32[2,1,16,40,512]{4,3,2,1,0:T(8,128)S(1)}, f32[2,1,16,40,512]{4,3,2,1,0:T(8,128)}) fusion(f32[2,2,16,40,512]{4,3,2,1,0:T(8,128)} %bitcast.614, s32[]{:T(128)S(6)} %select_n.89, s32[]{:T(128)S(6)} %select_n.87), kind=kLoop, calls=%fused_computation.329 | loop fusion | bytes 10485768 | tf_op jit(solution)/shard_map/jit(dynamic_index_in_dim)/dynamic_slice | solution.py:109
  13.9 4.4 %broadcast_multiply_fusion = (f32[4,16,8,16,16]{4,3,2,1,0:T(8,128)}, f32[4,16,8,16,16]{4,3,2,1,0:T(8,128)}) fusion(f32[4,8,16]{2,1,0:T(8,128)S(1)} %bitcast.637, f32[16,16]{1,0:T(8,128)S(1)} %fusion.165, f32[4,8,16]{2,1,0:T(8,128)S(1)} %bitcast.638), kind=kLoop, calls=%fused_computation.37 | loop fusion | flops 262144 | bytes 1053696 | tf_op jit(solution)/shard_map/mul | solution.py:145
  18.3 4.7 %mul.115 = f32[512,256]{1,0:T(8,128)} reshape(f32[4,16,8,16,16]{4,3,2,1,0:T(8,128)} %get-tuple-element.52) | data formatting | bytes 1048576 | tf_op jit(solution)/shard_map/mul | solution.py:145
  26.9 6.3 %fusion.31 = f32[1280,1024]{1,0:T(8,128)S(1)} fusion(f32[1280,512]{1,0:T(8,128)S(1)} %bitcast.611, f32[2,512,1024]{2,1,0:T(8,128)} %constant.195.clone, s32[]{:T(128)S(6)} %select_n.84), kind=kOutput, calls=%fused_computation.35 | convolution fusion | flops 4026531840 | bytes 9961476 | tf_op jit(solution)/shard_map/dot_general | solution.py:117
  33.2 32.4 %collective-permute-done = f32[40,2,16,512]{3,2,1,0:T(8,128)} collective-permute-done((f32[40,2,16,512]{3,2,1,0:T(8,128)}, f32[40,2,16,512]{3,2,1,0:T(8,128)}, u32[]{:S(2)}, u32[]{:S(2)}) %collective-permute-start) | collective-permute-done | bytes 2621472 | tf_op jit(solution)/shard_map/ppermute | solution.py:31
  65.7 6.3 %convolution_add_fusion = f32[1280,1024]{1,0:T(8,128)S(1)} fusion(f32[1280,1024]{1,0:T(8,128)S(1)} %fusion.31, f32[1280,512]{1,0:T(8,128)} %bitcast.11, f32[2,512,1024]{2,1,0:T(8,128)S(1)} %copy-done.3, s32[]{:T(128)S(6)} %select_n.89), kind=kOutput, calls=%fused_computation | convolution fusion | flops 4027842560 | bytes 15204356 | tf_op jit(solution)/shard_map/dot_general | solution.py:117
  93.6 5.0 %collective-permute-start.18 = (f32[5,2,16,1024]{3,2,1,0:T(8,128)S(1)}, f32[5,2,16,1024]{3,2,1,0:T(8,128)S(1)}, u32[]{:S(2)}, u32[]{:S(2)}) collective-permute-start(f32[5,2,16,1024]{3,2,1,0:T(8,128)S(1)} %bitcast.636), channel_id=1, source_target_pairs={{2,0},{4,2},{6,4},{3,1},{5,3},{7,5},{10,8},{12,10},{14,12},{11,9},... | collective-permute-start | bytes 1966088 | tf_op jit(solution)/shard_map/ppermute | solution.py:129
  101.5 6.6 %fusion.42 = f32[512,512]{1,0:T(8,128)S(1)} fusion(f32[512,512]{1,0:T(8,128)S(1)} %fusion.193, f32[512,256]{1,0:T(8,128)S(1)} %copy-done.6, f32[256,512]{1,0:T(8,128)S(1)} %collective-permute-done.14), kind=kOutput, calls=%fused_computation.58 | convolution fusion | flops 419692544 | bytes 3145728 | tf_op jit(solution)/shard_map/dot_general | solution.py:174
  112.7 6.4 %fusion.40 = f32[512,512]{1,0:T(8,128)S(1)} fusion(f32[512,512]{1,0:T(8,128)S(1)} %fusion.192, f32[512,256]{1,0:T(8,128)S(1)} %copy-done.6, f32[256,512]{1,0:T(8,128)S(1)} %collective-permute-done.10), kind=kOutput, calls=%fused_computation.56 | convolution fusion | flops 419692544 | bytes 3145728 | tf_op jit(solution)/shard_map/dot_general | solution.py:174
  119.7 4.2 %collective-permute-done.6 = f32[256,512]{1,0:T(8,128)S(1)} collective-permute-done((f32[256,512]{1,0:T(8,128)S(1)}, f32[256,512]{1,0:T(8,128)S(1)}, u32[]{:S(2)}, u32[]{:S(2)}) %collective-permute-start.6) | collective-permute-done | bytes 524320 | tf_op jit(solution)/shard_map/ppermute | solution.py:31
  123.9 6.4 %fusion.38 = f32[512,512]{1,0:T(8,128)S(1)} fusion(f32[512,512]{1,0:T(8,128)S(1)} %fusion.191, f32[512,256]{1,0:T(8,128)S(1)} %copy-done.6, f32[256,512]{1,0:T(8,128)S(1)} %collective-permute-done.6), kind=kOutput, calls=%fused_computation.54 | convolution fusion | flops 419692544 | bytes 3145728 | tf_op jit(solution)/shard_map/dot_general | solution.py:174
  132.7 3.7 %shard_map.95 = f32[8,2,16,1024]{3,2,1,0:T(8,128)S(1)} custom-call(s32[8]{0:T(128)S(1)} %get-tuple-element.54.starts_ref, f32[360]{0:T(512)S(1)} %reshape.136.weights_ref, f32[9,16,1024]{2,1,0:T(8,128)S(1)} %broadcast_multiply_fusion.2.factor_ref, f32[18,2,16,1024]{3,2,1,0:T(8,128)S(1)} %pad_maximum_fusion.1.refs_0_.refs_1_.refs_2_.refs_3_.refs_4_, ...), custom_call_target="tpu_custom_call" | custom-call | flops 230686720 | bytes 6291456 | tf_op jit(solution)/shard_map/pallas_call | solution.py:66
  147.4 18.0 %collective-permute-done.19 = f32[256,512]{1,0:T(8,128)S(1)} collective-permute-done((f32[256,512]{1,0:T(8,128)S(1)}, f32[256,512]{1,0:T(8,128)S(1)}, u32[]{:S(2)}, u32[]{:S(2)}) %collective-permute-start.19) | collective-permute-done | bytes 524320 | tf_op jit(solution)/shard_map/ppermute | solution.py:31
  165.4 6.4 %fusion.44 = f32[512,512]{1,0:T(8,128)S(1)} fusion(f32[512,512]{1,0:T(8,128)S(1)} %fusion.194, f32[512,256]{1,0:T(8,128)S(1)} %copy-done.6, f32[256,512]{1,0:T(8,128)S(1)} %collective-permute-done.19), kind=kOutput, calls=%fused_computation.60 | convolution fusion | flops 419692544 | bytes 3145728 | tf_op jit(solution)/shard_map/dot_general | solution.py:174
  172.0 6.6 %fusion.36 = f32[512,512]{1,0:T(8,128)S(1)} fusion(f32[512,512]{1,0:T(8,128)S(1)} %fusion.190, f32[512,256]{1,0:T(8,128)S(1)} %copy-done.6, f32[256,512]{1,0:T(8,128)S(1)} %collective-permute-done.2), kind=kOutput, calls=%fused_computation.52 | convolution fusion | flops 419692544 | bytes 3145728 | tf_op jit(solution)/shard_map/dot_general | solution.py:174
  187.3 23.0 %collective-permute-done.4 = f32[8,2,8,512]{3,0,2,1:T(8,128)S(1)} collective-permute-done((f32[8,2,8,512]{3,0,2,1:T(8,128)S(1)}, f32[8,2,8,512]{3,0,2,1:T(8,128)S(1)}, u32[]{:S(2)}, u32[]{:S(2)}) %collective-permute-start.4) | collective-permute-done | bytes 262176 | tf_op jit(solution)/shard_map/ppermute | solution.py:31
  210.2 6.1 %collective-permute-start.12 = (f32[8,2,8,512]{3,0,2,1:T(8,128)S(1)}, f32[8,2,8,512]{3,0,2,1:T(8,128)S(1)}, u32[]{:S(2)}, u32[]{:S(2)}) collective-permute-start(f32[8,2,8,512]{3,0,2,1:T(8,128)S(1)} %copy.53), channel_id=1, source_target_pairs={{0,16},{8,24},{16,0},{24,8},{1,17},{9,25},{17,1},{25,9},{2,18},{10... | collective-permute-start | bytes 786440 | tf_op jit(solution)/shard_map/ppermute | solution.py:31
  216.9 9.2 %collective-permute-done.8 = f32[8,2,8,512]{3,0,2,1:T(8,128)S(1)} collective-permute-done((f32[8,2,8,512]{3,0,2,1:T(8,128)S(1)}, f32[8,2,8,512]{3,0,2,1:T(8,128)S(1)}, u32[]{:S(2)}, u32[]{:S(2)}) %collective-permute-start.8) | collective-permute-done | bytes 262176 | tf_op jit(solution)/shard_map/ppermute | solution.py:31
  229.2 6.6 %collective-permute-done.9 = f32[8,2,8,512]{3,0,2,1:T(8,128)S(1)} collective-permute-done((f32[8,2,8,512]{3,0,2,1:T(8,128)S(1)}, f32[8,2,8,512]{3,0,2,1:T(8,128)S(1)}, u32[]{:S(2)}, u32[]{:S(2)}) %collective-permute-start.9) | collective-permute-done | bytes 262176 | tf_op jit(solution)/shard_map/ppermute | solution.py:31
  236.3 6.6 %collective-permute-done.11 = f32[8,2,8,512]{3,0,2,1:T(8,128)S(1)} collective-permute-done((f32[8,2,8,512]{3,0,2,1:T(8,128)S(1)}, f32[8,2,8,512]{3,0,2,1:T(8,128)S(1)}, u32[]{:S(2)}, u32[]{:S(2)}) %collective-permute-start.11) | collective-permute-done | bytes 262176 | tf_op jit(solution)/shard_map/ppermute | solution.py:31
  244.8 9.3 %collective-permute-done.12 = f32[8,2,8,512]{3,0,2,1:T(8,128)S(1)} collective-permute-done((f32[8,2,8,512]{3,0,2,1:T(8,128)S(1)}, f32[8,2,8,512]{3,0,2,1:T(8,128)S(1)}, u32[]{:S(2)}, u32[]{:S(2)}) %collective-permute-start.12) | collective-permute-done | bytes 262176 | tf_op jit(solution)/shard_map/ppermute | solution.py:31
  260.7 9.3 %collective-permute-done.17 = f32[8,2,8,512]{3,0,2,1:T(8,128)S(1)} collective-permute-done((f32[8,2,8,512]{3,0,2,1:T(8,128)S(1)}, f32[8,2,8,512]{3,0,2,1:T(8,128)S(1)}, u32[]{:S(2)}, u32[]{:S(2)}) %collective-permute-start.17) | collective-permute-done | bytes 262176 | tf_op jit(solution)/shard_map/ppermute | solution.py:31
  271.0 8.5 %collective-permute-done.21 = f32[8,2,8,512]{3,0,2,1:T(8,128)S(1)} collective-permute-done((f32[8,2,8,512]{3,0,2,1:T(8,128)S(1)}, f32[8,2,8,512]{3,0,2,1:T(8,128)S(1)}, u32[]{:S(2)}, u32[]{:S(2)}) %collective-permute-start.21) | collective-permute-done | bytes 262176 | tf_op jit(solution)/shard_map/ppermute | solution.py:31
  279.5 4.6 %collective-permute-done.22 = f32[8,2,8,512]{3,0,2,1:T(8,128)S(1)} collective-permute-done((f32[8,2,8,512]{3,0,2,1:T(8,128)S(1)}, f32[8,2,8,512]{3,0,2,1:T(8,128)S(1)}, u32[]{:S(2)}, u32[]{:S(2)}) %collective-permute-start.22) | collective-permute-done | bytes 262176 | tf_op jit(solution)/shard_map/ppermute | solution.py:31
  (133 shorter events, 79.3 us)
Async XLA Ops:
  7.6 58.0 %collective-permute-start = (f32[40,2,16,512]{3,2,1,0:T(8,128)}, f32[40,2,16,512]{3,2,1,0:T(8,128)}, u32[]{:S(2)}, u32[]{:S(2)}) collective-permute-start(f32[40,2,16,512]{3,2,1,0:T(8,128)} %bitcast.585), channel_id=1, source_target_pairs={{0,1},{1,0},{2,3},{3,2},{4,5},{5,4},{6,7},{7,6},{8,9},{9,8},{10,11... | collective-permute-start | bytes 7864328 | tf_op jit(solution)/shard_map/ppermute | solution.py:31
  89.5 11.9 %collective-permute-start.14 = (f32[256,512]{1,0:T(8,128)S(1)}, f32[256,512]{1,0:T(8,128)S(1)}, u32[]{:S(2)}, u32[]{:S(2)}) collective-permute-start(f32[256,512]{1,0:T(8,128)S(1)} %fusion.2), channel_id=1, source_target_pairs={{0,1},{1,0},{2,3},{3,2},{4,5},{5,4},{6,7},{7,6},{8,9},{9,8},{10,11... | collective-permute-start | bytes 1572872 | tf_op jit(solution)/shard_map/ppermute | solution.py:31
  90.8 21.9 %collective-permute-start.10 = (f32[256,512]{1,0:T(8,128)S(1)}, f32[256,512]{1,0:T(8,128)S(1)}, u32[]{:S(2)}, u32[]{:S(2)}) collective-permute-start(f32[256,512]{1,0:T(8,128)S(1)} %fusion.4), channel_id=1, source_target_pairs={{0,1},{1,0},{2,3},{3,2},{4,5},{5,4},{6,7},{7,6},{8,9},{9,8},{10,11... | collective-permute-start | bytes 1572872 | tf_op jit(solution)/shard_map/ppermute | solution.py:31
  91.1 32.9 %collective-permute-start.6 = (f32[256,512]{1,0:T(8,128)S(1)}, f32[256,512]{1,0:T(8,128)S(1)}, u32[]{:S(2)}, u32[]{:S(2)}) collective-permute-start(f32[256,512]{1,0:T(8,128)S(1)} %fusion.6), channel_id=1, source_target_pairs={{0,1},{1,0},{2,3},{3,2},{4,5},{5,4},{6,7},{7,6},{8,9},{9,8},{10,11... | collective-permute-start | bytes 1572872 | tf_op jit(solution)/shard_map/ppermute | solution.py:31
  92.3 46.5 %collective-permute-start.1 = (f32[5,2,16,1024]{3,2,1,0:T(8,128)S(1)}, f32[5,2,16,1024]{3,2,1,0:T(8,128)S(1)}, u32[]{:S(2)}, u32[]{:S(2)}) collective-permute-start(f32[5,2,16,1024]{3,2,1,0:T(8,128)S(1)} %bitcast.635), channel_id=1, source_target_pairs={{0,2},{2,4},{4,6},{1,3},{3,5},{5,7},{8,10},{10,12},{12,14},{9,11},... | collective-permute-start | bytes 1966088 | tf_op jit(solution)/shard_map/ppermute | solution.py:128
  93.6 38.8 %collective-permute-start.18 = (f32[5,2,16,1024]{3,2,1,0:T(8,128)S(1)}, f32[5,2,16,1024]{3,2,1,0:T(8,128)S(1)}, u32[]{:S(2)}, u32[]{:S(2)}) collective-permute-start(f32[5,2,16,1024]{3,2,1,0:T(8,128)S(1)} %bitcast.636), channel_id=1, source_target_pairs={{2,0},{4,2},{6,4},{3,1},{5,3},{7,5},{10,8},{12,10},{14,12},{11,9},... | collective-permute-start | bytes 1966088 | tf_op jit(solution)/shard_map/ppermute | solution.py:129
  108.7 73.2 %collective-permute-start.15 = (f32[8,2,8,512]{3,0,2,1:T(8,128)S(1)}, f32[8,2,8,512]{3,0,2,1:T(8,128)S(1)}, u32[]{:S(2)}, u32[]{:S(2)}) collective-permute-start(f32[8,2,8,512]{3,0,2,1:T(8,128)S(1)} %copy.58), channel_id=1, source_target_pairs={{0,8},{8,16},{16,24},{24,0},{1,9},{9,17},{17,25},{25,1},{2,10},{10... | collective-permute-start | bytes 786440 | tf_op jit(solution)/shard_map/ppermute | solution.py:31
  130.9 52.2 %collective-permute-start.7 = (f32[8,2,8,512]{3,0,2,1:T(8,128)S(1)}, f32[8,2,8,512]{3,0,2,1:T(8,128)S(1)}, u32[]{:S(2)}, u32[]{:S(2)}) collective-permute-start(f32[8,2,8,512]{3,0,2,1:T(8,128)S(1)} %copy.46), channel_id=1, source_target_pairs={{0,8},{8,16},{16,24},{24,0},{1,9},{9,17},{17,25},{25,1},{2,10},{10... | collective-permute-start | bytes 786440 | tf_op jit(solution)/shard_map/ppermute | solution.py:31
  143.5 28.5 %collective-permute-start.2 = (f32[256,512]{1,0:T(8,128)S(1)}, f32[256,512]{1,0:T(8,128)S(1)}, u32[]{:S(2)}, u32[]{:S(2)}) collective-permute-start(f32[256,512]{1,0:T(8,128)S(1)} %fusion.8), channel_id=1, source_target_pairs={{0,1},{1,0},{2,3},{3,2},{4,5},{5,4},{6,7},{7,6},{8,9},{9,8},{10,11... | collective-permute-start | bytes 1572872 | tf_op jit(solution)/shard_map/ppermute | solution.py:31
  144.8 20.7 %collective-permute-start.19 = (f32[256,512]{1,0:T(8,128)S(1)}, f32[256,512]{1,0:T(8,128)S(1)}, u32[]{:S(2)}, u32[]{:S(2)}) collective-permute-start(f32[256,512]{1,0:T(8,128)S(1)} %fusion), channel_id=1, source_target_pairs={{0,1},{1,0},{2,3},{3,2},{4,5},{5,4},{6,7},{7,6},{8,9},{9,8},{10,11... | collective-permute-start | bytes 1572872 | tf_op jit(solution)/shard_map/ppermute | solution.py:31
  179.2 5.6 %collective-permute-start.3 = (f32[8,2,8,512]{3,0,2,1:T(8,128)S(1)}, f32[8,2,8,512]{3,0,2,1:T(8,128)S(1)}, u32[]{:S(2)}, u32[]{:S(2)}) collective-permute-start(f32[8,2,8,512]{3,0,2,1:T(8,128)S(1)} %copy.40), channel_id=1, source_target_pairs={{0,8},{8,16},{16,24},{24,0},{1,9},{9,17},{17,25},{25,1},{2,10},{10... | collective-permute-start | bytes 786440 | tf_op jit(solution)/shard_map/ppermute | solution.py:31
  180.6 29.7 %collective-permute-start.4 = (f32[8,2,8,512]{3,0,2,1:T(8,128)S(1)}, f32[8,2,8,512]{3,0,2,1:T(8,128)S(1)}, u32[]{:S(2)}, u32[]{:S(2)}) collective-permute-start(f32[8,2,8,512]{3,0,2,1:T(8,128)S(1)} %copy.41), channel_id=1, source_target_pairs={{0,16},{8,24},{16,0},{24,8},{1,17},{9,25},{17,1},{25,9},{2,18},{10... | collective-permute-start | bytes 786440 | tf_op jit(solution)/shard_map/ppermute | solution.py:31
  181.5 34.8 %collective-permute-start.5 = (f32[8,2,8,512]{3,0,2,1:T(8,128)S(1)}, f32[8,2,8,512]{3,0,2,1:T(8,128)S(1)}, u32[]{:S(2)}, u32[]{:S(2)}) collective-permute-start(f32[8,2,8,512]{3,0,2,1:T(8,128)S(1)} %copy.42), channel_id=1, source_target_pairs={{0,24},{8,0},{16,8},{24,16},{1,25},{9,1},{17,9},{25,17},{2,26},{10... | collective-permute-start | bytes 786440 | tf_op jit(solution)/shard_map/ppermute | solution.py:31
  181.9 44.2 %collective-permute-start.8 = (f32[8,2,8,512]{3,0,2,1:T(8,128)S(1)}, f32[8,2,8,512]{3,0,2,1:T(8,128)S(1)}, u32[]{:S(2)}, u32[]{:S(2)}) collective-permute-start(f32[8,2,8,512]{3,0,2,1:T(8,128)S(1)} %copy.47), channel_id=1, source_target_pairs={{0,16},{8,24},{16,0},{24,8},{1,17},{9,25},{17,1},{25,9},{2,18},{10... | collective-permute-start | bytes 786440 | tf_op jit(solution)/shard_map/ppermute | solution.py:31
  183.2 52.6 %collective-permute-start.9 = (f32[8,2,8,512]{3,0,2,1:T(8,128)S(1)}, f32[8,2,8,512]{3,0,2,1:T(8,128)S(1)}, u32[]{:S(2)}, u32[]{:S(2)}) collective-permute-start(f32[8,2,8,512]{3,0,2,1:T(8,128)S(1)} %copy.48), channel_id=1, source_target_pairs={{0,24},{8,0},{16,8},{24,16},{1,25},{9,1},{17,9},{25,17},{2,26},{10... | collective-permute-start | bytes 786440 | tf_op jit(solution)/shard_map/ppermute | solution.py:31
  184.8 58.1 %collective-permute-start.11 = (f32[8,2,8,512]{3,0,2,1:T(8,128)S(1)}, f32[8,2,8,512]{3,0,2,1:T(8,128)S(1)}, u32[]{:S(2)}, u32[]{:S(2)}) collective-permute-start(f32[8,2,8,512]{3,0,2,1:T(8,128)S(1)} %copy.52), channel_id=1, source_target_pairs={{0,8},{8,16},{16,24},{24,0},{1,9},{9,17},{17,25},{25,1},{2,10},{10... | collective-permute-start | bytes 786440 | tf_op jit(solution)/shard_map/ppermute | solution.py:31
  210.2 43.9 %collective-permute-start.12 = (f32[8,2,8,512]{3,0,2,1:T(8,128)S(1)}, f32[8,2,8,512]{3,0,2,1:T(8,128)S(1)}, u32[]{:S(2)}, u32[]{:S(2)}) collective-permute-start(f32[8,2,8,512]{3,0,2,1:T(8,128)S(1)} %copy.53), channel_id=1, source_target_pairs={{0,16},{8,24},{16,0},{24,8},{1,17},{9,25},{17,1},{25,9},{2,18},{10... | collective-permute-start | bytes 786440 | tf_op jit(solution)/shard_map/ppermute | solution.py:31
  216.3 40.6 %collective-permute-start.13 = (f32[8,2,8,512]{3,0,2,1:T(8,128)S(1)}, f32[8,2,8,512]{3,0,2,1:T(8,128)S(1)}, u32[]{:S(2)}, u32[]{:S(2)}) collective-permute-start(f32[8,2,8,512]{3,0,2,1:T(8,128)S(1)} %copy.54), channel_id=1, source_target_pairs={{0,24},{8,0},{16,8},{24,16},{1,25},{9,1},{17,9},{25,17},{2,26},{10... | collective-permute-start | bytes 786440 | tf_op jit(solution)/shard_map/ppermute | solution.py:31
  226.1 34.6 %collective-permute-start.16 = (f32[8,2,8,512]{3,0,2,1:T(8,128)S(1)}, f32[8,2,8,512]{3,0,2,1:T(8,128)S(1)}, u32[]{:S(2)}, u32[]{:S(2)}) collective-permute-start(f32[8,2,8,512]{3,0,2,1:T(8,128)S(1)} %copy.59), channel_id=1, source_target_pairs={{0,16},{8,24},{16,0},{24,8},{1,17},{9,25},{17,1},{25,9},{2,18},{10... | collective-permute-start | bytes 786440 | tf_op jit(solution)/shard_map/ppermute | solution.py:31
  235.8 34.2 %collective-permute-start.17 = (f32[8,2,8,512]{3,0,2,1:T(8,128)S(1)}, f32[8,2,8,512]{3,0,2,1:T(8,128)S(1)}, u32[]{:S(2)}, u32[]{:S(2)}) collective-permute-start(f32[8,2,8,512]{3,0,2,1:T(8,128)S(1)} %copy.60), channel_id=1, source_target_pairs={{0,24},{8,0},{16,8},{24,16},{1,25},{9,1},{17,9},{25,17},{2,26},{10... | collective-permute-start | bytes 786440 | tf_op jit(solution)/shard_map/ppermute | solution.py:31
  235.8 49.5 %copy-start.1 = (f32[32,9]{0,1:T(8,128)S(1)}, f32[32,9]{0,1:T(8,128)}, u32[]{:S(2)}) copy-start(f32[32,9]{0,1:T(8,128)} %param.13) | copy-start | bytes 3460
  242.9 28.1 %collective-permute-start.20 = (f32[8,2,8,512]{3,0,2,1:T(8,128)S(1)}, f32[8,2,8,512]{3,0,2,1:T(8,128)S(1)}, u32[]{:S(2)}, u32[]{:S(2)}) collective-permute-start(f32[8,2,8,512]{3,0,2,1:T(8,128)S(1)} %copy.64), channel_id=1, source_target_pairs={{0,8},{8,16},{16,24},{24,0},{1,9},{9,17},{17,25},{25,1},{2,10},{10... | collective-permute-start | bytes 786440 | tf_op jit(solution)/shard_map/ppermute | solution.py:31
  254.2 25.3 %collective-permute-start.21 = (f32[8,2,8,512]{3,0,2,1:T(8,128)S(1)}, f32[8,2,8,512]{3,0,2,1:T(8,128)S(1)}, u32[]{:S(2)}, u32[]{:S(2)}) collective-permute-start(f32[8,2,8,512]{3,0,2,1:T(8,128)S(1)} %copy.65), channel_id=1, source_target_pairs={{0,16},{8,24},{16,0},{24,8},{1,17},{9,25},{17,1},{25,9},{2,18},{10... | collective-permute-start | bytes 786440 | tf_op jit(solution)/shard_map/ppermute | solution.py:31
  257.0 27.1 %collective-permute-start.22 = (f32[8,2,8,512]{3,0,2,1:T(8,128)S(1)}, f32[8,2,8,512]{3,0,2,1:T(8,128)S(1)}, u32[]{:S(2)}, u32[]{:S(2)}) collective-permute-start(f32[8,2,8,512]{3,0,2,1:T(8,128)S(1)} %copy.66), channel_id=1, source_target_pairs={{0,24},{8,0},{16,8},{24,16},{1,25},{9,1},{17,9},{25,17},{2,26},{10... | collective-permute-start | bytes 786440 | tf_op jit(solution)/shard_map/ppermute | solution.py:31
  (10 other events, 137.7 us)
